TPU v7x, 256 devices: a whole 4x4x8 slice. The times are simulated.
256 devices in a mesh: blk: 64 (over y, z, core), sub: 4 (over x).
Axes of the slice: x: 4, y: 4, z: 8, core: 2. Of those that a mesh axis runs over, the one named last changes fastest.
Arguments:
- residual_rhs: float32 [6, 196608], P(None, ('blk', 'sub')), may hold values from -6 to 6
- diag_blocks: bfloat16 [6, 6, 196608], P(None, None, ('blk', 'sub')), may hold values from -1.5 to 6, as said below
- jacobian_blocks: bfloat16 [6, 6, 6, 196608], P(None, None, None, ('blk', 'sub')), may hold values from -1.5 to 1.5
- neighbors: int32 [6, 196608], P(None, ('blk', 'sub')), may hold values from 0 to 1535, as said below
- partner: int32 [64], replicated, may hold values from 0 to 63, as said below
- fringe_source: int32 [131072], P(('blk', 'sub')), may hold values from 0 to 767
- fringe_weight: float32 [131072], P(('blk', 'sub')), may hold values from 0.5 to 2
- fringe_donor: int32 [131072], P(('blk', 'sub')), may hold values from 0 to 511
- metric_sens: bfloat16 [3, 6, 196608], P(None, None, ('blk', 'sub')), may hold values from -6 to 6
- warp_row: int32 [524288], P(('blk', 'sub')), may hold values from 0 to 767
- warp_node: int32 [524288], P(('blk', 'sub')), may hold values from 0 to 8191
- warp_weight: float32 [524288], P(('blk', 'sub')), may hold values from 0.05 to 0.3
Outputs:
- adjoint_state: float32 [6, 196608], P(None, ('blk', 'sub'))
- surface_sens: float32 [3, 8192], P(None, 'blk')
Inputs may be any that keep to these rules, and one draw needn't show every extreme that they name: `neighbors`: indices into the window: below 256 the lower rim, then 768 own rows, then 256 upper rim, then 256 partner rows. partner[partner[b]] = b and partner[b] != b. `diag_blocks`: each block's diagonal entries are 2.5 or more.
All inputs are finite; a program needn't handle non-finite values.
Results may differ from a plain program's by a relative error of at most 0.0003.
Values sent between devices are 32-bit elements; how exact they have to be, the bound alone decides.
A program may use at most 128 MiB of HBM per device.

v0:
```python
import jax
import jax.numpy as jnp
from jax import lax
from jax.sharding import PartitionSpec as P

SWEEPS = 3
CELLS_DEV = 512
RIM = 256
NODE_BLK = 128


relaxation = 0.8


def with_halo(value, sides, width):
    for axis, dim in sides:
        peers, length = (lax.axis_size(axis), value.shape[dim])
        up = [(i, (i + 1) % peers) for i in range(peers - 1)]
        down = [(j, i) for i, j in up]
        last = lax.slice_in_dim(value, length - width, length, axis=dim)
        first = lax.slice_in_dim(value, 0, width, axis=dim)
        before = lax.ppermute(last, axis, up)
        after = lax.ppermute(first, axis, down)
        value = jnp.concatenate([before, value, after], axis=dim)
    return value


def body(
    residual_rhs,
    diag_blocks,
    jacobian_blocks,
    neighbors,
    partner,
    fringe_source,
    fringe_weight,
    fringe_donor,
    metric_sens,
    warp_row,
    warp_node,
    warp_weight,
):
    field_count = residual_rhs.shape[0]
    row_count = residual_rhs.shape[1]
    cell_count = CELLS_DEV
    migrant_count = row_count - cell_count
    groups = lax.axis_size("blk")
    own_group = lax.axis_index("blk")
    mate_group = partner[own_group]
    pivots = jnp.stack([diag_blocks[f, f] for f in range(field_count)]).astype(jnp.float32)
    state = relaxation * residual_rhs / pivots
    for sweep in range(SWEEPS):
        edges = with_halo(state[:, :cell_count], ((("blk", "sub"), 1),), RIM)
        migrants = state[:, cell_count:]
        every = lax.all_gather(migrants, "blk", axis=1, tiled=True)
        mates = lax.dynamic_slice_in_dim(every, mate_group * migrant_count, migrant_count, 1)
        outgoing = state[:, fringe_source] * fringe_weight[None, :]
        arrived = lax.all_to_all(outgoing, "blk", split_axis=1, concat_axis=1, tiled=True)
        window = jnp.concatenate(
            [edges[:, :RIM], state, edges[:, RIM + cell_count :], mates], axis=1
        )
        image = jnp.zeros((field_count, row_count), jnp.float32)
        for apply_f in range(field_count):
            image = image + diag_blocks[apply_f].astype(jnp.float32) * state[apply_f][None, :]
        for k in range(jacobian_blocks.shape[0]):
            picked = window[:, neighbors[k]]
            for apply_f in range(field_count):
                image = (
                    image
                    + jacobian_blocks[k, apply_f].astype(jnp.float32) * picked[apply_f][None, :]
                )
        image = image.at[:, fringe_donor].add(-arrived)
        state = state + relaxation * (residual_rhs - image) / pivots
    volume = jnp.zeros((3, row_count), jnp.float32)
    for f in range(field_count):
        volume = volume + metric_sens[:, f].astype(jnp.float32) * state[f][None, :]
    terms = volume[:, warp_row] * warp_weight[None, :]
    dense = jnp.zeros((3, groups * NODE_BLK), jnp.float32).at[:, warp_node].add(terms)
    total = lax.psum(dense, ("blk", "sub"))
    surface = lax.dynamic_slice_in_dim(total, own_group * NODE_BLK, NODE_BLK, 1)
    return (state, surface)


def solution(mesh):
    in_specs = (
        P(None, ("blk", "sub")),
        P(None, None, ("blk", "sub")),
        P(None, None, None, ("blk", "sub")),
        P(None, ("blk", "sub")),
        P(),
        P(("blk", "sub")),
        P(("blk", "sub")),
        P(("blk", "sub")),
        P(None, None, ("blk", "sub")),
        P(("blk", "sub")),
        P(("blk", "sub")),
        P(("blk", "sub")),
    )
    out_specs = (P(None, ("blk", "sub")), P(None, "blk"))
    return jax.shard_map(body, mesh=mesh, in_specs=in_specs, out_specs=out_specs, check_vma=False)
```

profile of v0, /device:TPU:1, one launch (start us, length us, event | category | flops | bytes accessed | tf_op | source)
XLA Modules:
  0.0 697.4 jit_solution(1942676058906816476)
XLA Ops:
  9.3 3.9 collective-permute-start
  13.3 3.7 collective-permute-start.1
  21.0 14.5 %all-to-all-start = ((f32[6,64,8]{0,2,1:T(8,128)}), f32[6,64,8]{0,2,1:T(8,128)}, u32[]{:S(2)}, u32[]{:S(2)}) async-start(f32[6,64,8]{0,2,1:T(8,128)} %bitcast_multiply_fusion.2), calls=%async_computation | async-start | bytes 524288 | tf_op jit(solution)/shard_map/all_to_all | solution.py:57
  35.5 1.8 slice_reduce_fusion.131
  37.5 62.1 %all_gather.9 = f32[6,16384]{0,1:T(8,128)} all-gather(f32[6,256]{0,1:T(8,128)S(1)} %get-tuple-element.191), channel_id=1, replica_groups=mesh['blk'=64,'sub'=4] {'blk'}, dimensions={1}, use_global_device_ids=true | all-gather | bytes 399360 | tf_op jit(solution)/shard_map/all_gather | solution.py:54
  140.4 1.8 gather_fusion
  142.3 1.8 slice_reduce_fusion.125
  144.1 1.6 gather_fusion.1
  145.6 1.8 slice_reduce_fusion.119
  147.4 1.6 gather_fusion.2
  149.0 1.8 slice_reduce_fusion.113
  150.8 1.6 gather_fusion.3
  152.4 1.8 slice_reduce_fusion.107
  154.2 1.8 gather_fusion.4
  156.0 1.8 slice_reduce_fusion.101
  157.8 1.8 gather_fusion.5
  161.0 10.4 %fusion.94 = f32[6,768]{0,1:T(8,128)S(1)} fusion(bf16[1,1,6,768]{2,3,1,0:T(8,128)(2,1)} %copy.260, bf16[1,1,6,768]{2,3,1,0:T(8,128)(2,1)} %copy.259, bf16[1,1,6,768]{2,3,1,0:T(8,128)(2,1)} %copy.258, bf16[1,1,6,768]{2,3,1,0:T(8,128)(2,1)} %copy.257, bf16[1,1,6,768]{2,3,1,0:T(8,128)(2,1)} %copy.256, bf16[1,1,6,768]{2,3,1,0:T(8,128)(2,1)} %copy.255, ...), kind=kLoop, calls=%fused_computation.253 | loop fusion | flops 576000 | bytes 534528 | tf_op jit(solution)/shard_map/add | solution.py:68
  171.4 3.9 scatter_custom_fusion
  175.4 1.8 slice_reduce_fusion.89
  178.2 54.6 %all_gather.10 = f32[6,16384]{0,1:T(8,128)S(1)} all-gather(f32[6,256]{0,1:T(8,128)S(1)} %get-tuple-element.188), channel_id=1, replica_groups=mesh['blk'=64,'sub'=4] {'blk'}, dimensions={1}, use_global_device_ids=true | all-gather | bytes 399360 | tf_op jit(solution)/shard_map/all_gather | solution.py:54
  232.8 1.9 collective-permute-start.2
  234.7 4.9 collective-permute-start.3
  240.5 18.2 %all-to-all-start.1 = ((f32[6,64,8]{0,2,1:T(8,128)}), f32[6,64,8]{0,2,1:T(8,128)}, u32[]{:S(2)}, u32[]{:S(2)}) async-start(f32[6,64,8]{0,2,1:T(8,128)} %bitcast_multiply_fusion.1), calls=%async_computation.1 | async-start | bytes 524288 | tf_op jit(solution)/shard_map/all_to_all | solution.py:57
  258.8 1.6 gather_fusion.7
  260.3 1.6 gather_fusion.8
  261.9 1.6 gather_fusion.9
  263.5 2.7 gather_fusion.10
  266.2 3.0 gather_fusion.11
  269.2 3.0 gather_fusion.12
  280.3 6.9 fusion.110
  287.2 4.1 scatter_custom_fusion.1
  291.4 1.8 slice_reduce_fusion.47
  294.3 57.2 %all_gather.11 = f32[6,16384]{0,1:T(8,128)S(1)} all-gather(f32[6,256]{0,1:T(8,128)S(1)} %get-tuple-element.185), channel_id=1, replica_groups=mesh['blk'=64,'sub'=4] {'blk'}, dimensions={1}, use_global_device_ids=true | all-gather | bytes 399360 | tf_op jit(solution)/shard_map/all_gather | solution.py:54
  351.5 1.9 collective-permute-start.4
  353.4 4.9 collective-permute-start.5
  359.1 9.6 %all-to-all-start.2 = ((f32[6,64,8]{0,2,1:T(8,128)}), f32[6,64,8]{0,2,1:T(8,128)}, u32[]{:S(2)}, u32[]{:S(2)}) async-start(f32[6,64,8]{0,2,1:T(8,128)} %bitcast_multiply_fusion), calls=%async_computation.2 | async-start | bytes 524288 | tf_op jit(solution)/shard_map/all_to_all | solution.py:57
  368.9 1.6 gather_fusion.14
  370.5 1.6 gather_fusion.15
  372.0 1.6 gather_fusion.16
  373.6 1.6 gather_fusion.17
  375.2 3.0 gather_fusion.18
  378.2 3.0 gather_fusion.19
  381.2 1.2 slice_reduce_fusion.41
  383.6 1.2 slice_reduce_fusion.29
  389.3 6.9 fusion.126
  396.3 4.3 scatter_custom_fusion.2
  402.8 20.1 %scatter_custom_fusion.3 = f32[3,8192]{0,1:T(8,128)} fusion(s32[2048]{0:T(1024)} %get-tuple-element.217, f32[]{:T(128)} %constant.7.clone.1, f32[2048]{0:T(1024)S(1)} %copy-done.112, f32[3,768]{0,1:T(8,128)S(1)} %fusion.130, s32[2048]{0:T(1024)S(1)} %copy-done.107), kind=kCustom, calls=%fused_computation.26 | custom fusion | flops 12288 | bytes 124416 | tf_op jit(solution)/shard_map/scatter-add | solution.py:77
  423.8 264.8 %all-reduce.2.cloned.1.call-done = f32[3,8192]{0,1:T(8,128)} async-done(((f32[3,8192]{0,1:T(8,128)}), f32[3,8192]{0,1:T(8,128)}) %all-reduce.2.cloned.1.call-update) | async-done | bytes 98320 | tf_op jit(solution)/shard_map/psum | solution.py:78
  (348 shorter events, 68.4 us)
Async XLA Ops:
  7.2 30.2 %copy-start.98 = (bf16[6,6,768]{2,1,0:T(8,128)(2,1)S(1)}, bf16[6,6,768]{2,1,0:T(8,128)(2,1)}, u32[]{:S(2)}) copy-start(bf16[6,6,768]{2,1,0:T(8,128)(2,1)} %param.13) | copy-start | bytes 165892
  7.2 30.2 %copy-start.97 = (bf16[6,6,6,768]{3,2,1,0:T(8,128)(2,1)S(1)}, bf16[6,6,6,768]{3,2,1,0:T(8,128)(2,1)}, u32[]{:S(2)}) copy-start(bf16[6,6,6,768]{3,2,1,0:T(8,128)(2,1)} %param.14) | copy-start | bytes 995332
  9.3 131.1 %collective-permute-start = (f32[6,256]{0,1:T(8,128)S(1)}, f32[6,256]{0,1:T(8,128)S(1)}, u32[]{:S(2)}, u32[]{:S(2)}) collective-permute-start(f32[6,256]{0,1:T(8,128)S(1)} %get-tuple-element.190), channel_id=1, source_target_pairs={{0,1},{1,2},{2,3},{3,4},{4,5},{5,6},{6,7},{7,8},{8,9},{9,10},{10,1... | collective-permute-start | bytes 18440 | tf_op jit(solution)/shard_map/ppermute | solution.py:22
  13.3 127.1 %collective-permute-start.1 = (f32[6,256]{0,1:T(8,128)S(1)}, f32[6,256]{0,1:T(8,128)S(1)}, u32[]{:S(2)}, u32[]{:S(2)}) collective-permute-start(f32[6,256]{0,1:T(8,128)S(1)} %get-tuple-element.192), channel_id=1, source_target_pairs={{1,0},{2,1},{3,2},{4,3},{5,4},{6,5},{7,6},{8,7},{9,8},{10,9},{11,1... | collective-permute-start | bytes 18440 | tf_op jit(solution)/shard_map/ppermute | solution.py:23
  20.1 79.4 %copy-start.94 = (f32[64,8]{1,0:T(8,128)}, f32[64,8]{1,0:T(8,128)S(1)}, u32[]{:S(2)}) copy-start(f32[64,8]{1,0:T(8,128)S(1)} %mul.1505) | copy-start | bytes 6148
  21.0 150.4 %all-to-all-start = ((f32[6,64,8]{0,2,1:T(8,128)}), f32[6,64,8]{0,2,1:T(8,128)}, u32[]{:S(2)}, u32[]{:S(2)}) async-start(f32[6,64,8]{0,2,1:T(8,128)} %bitcast_multiply_fusion.2), calls=%async_computation | async-start | bytes 524288 | tf_op jit(solution)/shard_map/all_to_all | solution.py:57
  37.4 62.2 %copy-start.116 = (s32[64]{0:T(128)S(1)}, s32[64]{0:T(128)}, u32[]{:S(2)}) copy-start(s32[64]{0:T(128)} %param.16) | copy-start | bytes 772
  37.4 63.4 %copy-start.111 = (s32[6,768]{1,0:T(8,128)S(1)}, s32[6,768]{1,0:T(8,128)}, u32[]{:S(2)}) copy-start(s32[6,768]{1,0:T(8,128)} %param.15) | copy-start | bytes 55300
  37.4 63.5 %copy-start.115 = (s32[512]{0:T(512)S(1)}, s32[512]{0:T(512)}, u32[]{:S(2)}) copy-start(s32[512]{0:T(512)} %param.19) | copy-start | bytes 6148
  37.4 64.0 %copy-start.100 = (bf16[3,6,768]{2,1,0:T(8,128)(2,1)S(1)}, bf16[3,6,768]{2,1,0:T(8,128)(2,1)}, u32[]{:S(2)}) copy-start(bf16[3,6,768]{2,1,0:T(8,128)(2,1)} %param.20) | copy-start | bytes 82948
  37.5 65.6 %copy-start.113 = (s32[2048]{0:T(1024)S(1)}, s32[2048]{0:T(1024)}, u32[]{:S(2)}) copy-start(s32[2048]{0:T(1024)} %param.22) | copy-start | bytes 24580
  37.5 65.6 %copy-start.114 = (s32[2048]{0:T(1024)S(1)}, s32[2048]{0:T(1024)}, u32[]{:S(2)}) copy-start(s32[2048]{0:T(1024)} %param.21) | copy-start | bytes 24580
  37.5 66.8 %copy-start.99 = (f32[6,768]{1,0:T(8,128)S(1)}, f32[6,768]{1,0:T(8,128)}, u32[]{:S(2)}) copy-start(f32[6,768]{1,0:T(8,128)} %param.12) | copy-start | bytes 55300
  104.9 56.0 %copy-start.2 = (bf16[1,1,6,768]{2,3,1,0:T(8,128)(2,1)}, bf16[1,1,6,768]{2,3,1,0:T(8,128)(2,1)S(1)}, u32[]{:S(2)}) copy-start(bf16[1,1,6,768]{2,3,1,0:T(8,128)(2,1)S(1)} %copy.241) | copy-start | bytes 27652
  104.9 30.4 %copy-start.106 = (bf16[3,1,768]{2,1,0:T(2,128)(2,1)S(1)}, bf16[3,1,768]{2,1,0:T(2,128)(2,1)}, u32[]{:S(2)}) copy-start(bf16[3,1,768]{2,1,0:T(2,128)(2,1)} %get-tuple-element.205) | copy-start | bytes 13828
  105.1 55.8 %copy-start.5 = (bf16[1,1,6,768]{2,3,1,0:T(8,128)(2,1)}, bf16[1,1,6,768]{2,3,1,0:T(8,128)(2,1)S(1)}, u32[]{:S(2)}) copy-start(bf16[1,1,6,768]{2,3,1,0:T(8,128)(2,1)S(1)} %copy.242) | copy-start | bytes 27652
  105.1 31.1 %copy-start.105 = (bf16[3,1,768]{2,1,0:T(2,128)(2,1)S(1)}, bf16[3,1,768]{2,1,0:T(2,128)(2,1)}, u32[]{:S(2)}) copy-start(bf16[3,1,768]{2,1,0:T(2,128)(2,1)} %get-tuple-element.208) | copy-start | bytes 13828
  105.3 55.6 %copy-start.8 = (bf16[1,1,6,768]{2,3,1,0:T(8,128)(2,1)}, bf16[1,1,6,768]{2,3,1,0:T(8,128)(2,1)S(1)}, u32[]{:S(2)}) copy-start(bf16[1,1,6,768]{2,3,1,0:T(8,128)(2,1)S(1)} %copy.243) | copy-start | bytes 27652
  105.3 31.7 %copy-start.104 = (bf16[3,1,768]{2,1,0:T(2,128)(2,1)S(1)}, bf16[3,1,768]{2,1,0:T(2,128)(2,1)}, u32[]{:S(2)}) copy-start(bf16[3,1,768]{2,1,0:T(2,128)(2,1)} %get-tuple-element.207) | copy-start | bytes 13828
  105.5 55.4 %copy-start.11 = (bf16[1,1,6,768]{2,3,1,0:T(8,128)(2,1)}, bf16[1,1,6,768]{2,3,1,0:T(8,128)(2,1)S(1)}, u32[]{:S(2)}) copy-start(bf16[1,1,6,768]{2,3,1,0:T(8,128)(2,1)S(1)} %copy.244) | copy-start | bytes 27652
  105.5 32.3 %copy-start.103 = (bf16[3,1,768]{2,1,0:T(2,128)(2,1)S(1)}, bf16[3,1,768]{2,1,0:T(2,128)(2,1)}, u32[]{:S(2)}) copy-start(bf16[3,1,768]{2,1,0:T(2,128)(2,1)} %get-tuple-element.206) | copy-start | bytes 13828
  105.7 55.3 %copy-start.14 = (bf16[1,1,6,768]{2,3,1,0:T(8,128)(2,1)}, bf16[1,1,6,768]{2,3,1,0:T(8,128)(2,1)S(1)}, u32[]{:S(2)}) copy-start(bf16[1,1,6,768]{2,3,1,0:T(8,128)(2,1)S(1)} %copy.245) | copy-start | bytes 27652
  105.7 33.0 %copy-start.102 = (bf16[3,1,768]{2,1,0:T(2,128)(2,1)S(1)}, bf16[3,1,768]{2,1,0:T(2,128)(2,1)}, u32[]{:S(2)}) copy-start(bf16[3,1,768]{2,1,0:T(2,128)(2,1)} %get-tuple-element.210) | copy-start | bytes 13828
  105.9 55.1 %copy-start.17 = (bf16[1,1,6,768]{2,3,1,0:T(8,128)(2,1)}, bf16[1,1,6,768]{2,3,1,0:T(8,128)(2,1)S(1)}, u32[]{:S(2)}) copy-start(bf16[1,1,6,768]{2,3,1,0:T(8,128)(2,1)S(1)} %copy.246) | copy-start | bytes 27652
  105.9 33.6 %copy-start.101 = (bf16[3,1,768]{2,1,0:T(2,128)(2,1)S(1)}, bf16[3,1,768]{2,1,0:T(2,128)(2,1)}, u32[]{:S(2)}) copy-start(bf16[3,1,768]{2,1,0:T(2,128)(2,1)} %get-tuple-element.209) | copy-start | bytes 13828
  171.4 5.8 copy-start.109
  178.2 61.4 %copy-start.95 = (f32[64,8]{1,0:T(8,128)S(1)}, f32[64,8]{1,0:T(8,128)}, u32[]{:S(2)}) copy-start(f32[64,8]{1,0:T(8,128)} %copy-done.94) | copy-start | bytes 6148
  232.8 25.9 %collective-permute-start.2 = (f32[6,256]{0,1:T(8,128)S(1)}, f32[6,256]{0,1:T(8,128)S(1)}, u32[]{:S(2)}, u32[]{:S(2)}) collective-permute-start(f32[6,256]{0,1:T(8,128)S(1)} %get-tuple-element.187), channel_id=1, source_target_pairs={{0,1},{1,2},{2,3},{3,4},{4,5},{5,6},{6,7},{7,8},{8,9},{9,10},{10,1... | collective-permute-start | bytes 18440 | tf_op jit(solution)/shard_map/ppermute | solution.py:22
  234.7 24.0 %collective-permute-start.3 = (f32[6,256]{0,1:T(8,128)S(1)}, f32[6,256]{0,1:T(8,128)S(1)}, u32[]{:S(2)}, u32[]{:S(2)}) collective-permute-start(f32[6,256]{0,1:T(8,128)S(1)} %get-tuple-element.189), channel_id=1, source_target_pairs={{1,0},{2,1},{3,2},{4,3},{5,4},{6,5},{7,6},{8,7},{9,8},{10,9},{11,1... | collective-permute-start | bytes 18440 | tf_op jit(solution)/shard_map/ppermute | solution.py:23
  240.5 46.7 %all-to-all-start.1 = ((f32[6,64,8]{0,2,1:T(8,128)}), f32[6,64,8]{0,2,1:T(8,128)}, u32[]{:S(2)}, u32[]{:S(2)}) async-start(f32[6,64,8]{0,2,1:T(8,128)} %bitcast_multiply_fusion.1), calls=%async_computation.1 | async-start | bytes 524288 | tf_op jit(solution)/shard_map/all_to_all | solution.py:57
  287.2 6.0 copy-start.110
  294.3 64.0 %copy-start.96 = (f32[64,8]{1,0:T(8,128)S(1)}, f32[64,8]{1,0:T(8,128)}, u32[]{:S(2)}) copy-start(f32[64,8]{1,0:T(8,128)} %copy-done.94) | copy-start | bytes 6148
  351.5 17.3 %collective-permute-start.4 = (f32[6,256]{0,1:T(8,128)S(1)}, f32[6,256]{0,1:T(8,128)S(1)}, u32[]{:S(2)}, u32[]{:S(2)}) collective-permute-start(f32[6,256]{0,1:T(8,128)S(1)} %get-tuple-element.184), channel_id=1, source_target_pairs={{0,1},{1,2},{2,3},{3,4},{4,5},{5,6},{6,7},{7,8},{8,9},{9,10},{10,1... | collective-permute-start | bytes 18440 | tf_op jit(solution)/shard_map/ppermute | solution.py:22
  353.4 15.4 %collective-permute-start.5 = (f32[6,256]{0,1:T(8,128)S(1)}, f32[6,256]{0,1:T(8,128)S(1)}, u32[]{:S(2)}, u32[]{:S(2)}) collective-permute-start(f32[6,256]{0,1:T(8,128)S(1)} %get-tuple-element.186), channel_id=1, source_target_pairs={{1,0},{2,1},{3,2},{4,3},{5,4},{6,5},{7,6},{8,7},{9,8},{10,9},{11,1... | collective-permute-start | bytes 18440 | tf_op jit(solution)/shard_map/ppermute | solution.py:23
  359.1 37.0 %all-to-all-start.2 = ((f32[6,64,8]{0,2,1:T(8,128)}), f32[6,64,8]{0,2,1:T(8,128)}, u32[]{:S(2)}, u32[]{:S(2)}) async-start(f32[6,64,8]{0,2,1:T(8,128)} %bitcast_multiply_fusion), calls=%async_computation.2 | async-start | bytes 524288 | tf_op jit(solution)/shard_map/all_to_all | solution.py:57
  368.7 319.8 %all-reduce.2.cloned.1.call-start = ((), (), s32[]{:S(2)}) async-start(), calls=%async_computation.3 | async-start | bytes 8388608 | tf_op jit(solution)/shard_map/psum | solution.py:78
  383.6 5.3 copy-start.81
  383.6 5.3 copy-start.83
  383.6 5.3 copy-start.85
  383.6 5.3 copy-start.87
  396.2 5.7 copy-start.88
  396.2 5.7 copy-start.89
  396.2 5.7 copy-start.90
  396.2 5.7 copy-start.91
  396.2 5.7 copy-start.92
  396.2 5.7 copy-start.93
  396.2 6.6 copy-start.107
  396.3 6.6 copy-start.112
  (79 other events, 320.4 us)
Sparse Core Ops, SparseCore 0:
  423.1 265.4 all-reduce.1
where the time goes:
time: 707 us; the launch traced here: 697 us
  waiting for transfers between devices  265 us (37%)
  blocking collectives  174 us (25%)
  local copies, waits for them, and re-layouts  114 us (16%)
  other arithmetic  63.8 us (9%)
  starting transfers between devices  63.6 us (9%)
  between operations  17.5 us (2%)
    psum x1, waiting for transfers between devices, body(): total = lax.psum(dense, ('blk', 'sub'))  265 us
    all_gather x3, blocking collectives, body(): every = lax.all_gather(migrants, 'blk', axis=1, tiled=True)  174 us
    all_to_all x3, starting transfers between devices, body(): lax.all_to_all(outgoing, 'blk', split_axis=1, concat_axis=1, tiled=True)  42.3 us
    gather x18, local copies, waits for them, and re-layouts, body(): picked = window[:, neighbors[k]]  35.8 us
    slice x38, local copies, waits for them, and re-layouts, body(): jacobian_blocks[k, apply_f].astype(jnp.float32) * picked[apply_f][None, :]  25.7 us
    slice x18, local copies, waits for them, and re-layouts, body(): picked[apply_f][None, :]  24.7 us
    add x3, other arithmetic, body(): image + jacobian_blocks[k, apply_f].astype(jnp.float32) * picked[apply_f]...  24.2 us
    scatter-add x1, other arithmetic, body(): jnp.zeros((3, groups * NODE_BLK), jnp.float32).at[:, warp_node].add(terms)  20.1 us
  transfers between devices with their start and end apart: 10, of which 1 were waited for; matrix products, arithmetic and copies ran while one was open for 19% of the time, Pallas kernels for 0%

commit v1 on v0

v1 whole, which is shorter than its diff:
```python
import jax
import jax.numpy as jnp
from jax import lax
from jax.experimental import pallas as pl
from jax.experimental.pallas import tpu as pltpu
from jax.sharding import PartitionSpec as P

MESH = pl.DeviceIdType.MESH
F32, BF16, I32 = jnp.float32, jnp.bfloat16, jnp.int32

FIELDS = 6
NEIGH = 6
SWEEPS = 3
ROWS = 768
CHUNKS = 6
RIM = 256
LANES = 128
GZ = 8
GR = 8
SUBS = 4
DEVICES = 256
WARP_CHUNKS = 16
RELAX = 0.8


def split3(v):
    a = v.astype(BF16).astype(F32)
    b = (v - a).astype(BF16).astype(F32)
    return a, b, v - a - b


def lane_pick(sources, first, low, high):
    acc = jnp.zeros((8, LANES), F32)
    for n, src in enumerate(sources):
        got = jnp.take_along_axis(src, low, axis=1, mode="promise_in_bounds")
        acc = jnp.where(high == first + n, got, acc)
    return acc


def row8(ref, i, start=0):
    return jnp.broadcast_to(ref[i : i + 1, start : start + LANES], (8, LANES))


def dot_nt(a, b):
    return lax.dot_general(a, b, (((1,), (1,)), ((), ())), preferred_element_type=F32)


def kernel(
    rhs, diag, jac, nbr, partner, fsrc, fwei, fdon, metric, wrow, wnode, wwei,
    out_state, out_surf,
    states, coef, image, fsi, fwt, don1h, low1h, whi,
    send1, recv1_0, recv1_1, recv1_2, send2, recv2_0, recv2_1, recv2_2, rims,
    volume, spread, send_a, recv_a, send_b, recv_b,
    sem_s1, sem_r1, sem_s2, sem_r2, sem_sr, sem_rl, sem_ru, sem_fin,
):
    blk, sub = lax.axis_index("blk"), lax.axis_index("sub")
    y, z, core = blk // 16, (blk // 2) % GZ, blk % 2
    r = core * 4 + y
    dev = blk * SUBS + sub
    after, before = (dev + 1) % DEVICES, (dev + DEVICES - 1) % DEVICES

    def blk_of(zz, rr):
        return (rr % 4) * 16 + zz * 2 + rr // 4

    barrier = pltpu.get_barrier_semaphore()

    def greet(b, s):
        pl.semaphore_signal(barrier, inc=1, device_id=(b, s), device_id_type=MESH)

    for j in range(1, GZ):
        greet(blk_of((z + j) % GZ, r), sub)
    for j in range(1, GR * SUBS):
        greet(blk_of(z, (r + j // SUBS) % GR), (sub + j % SUBS) % SUBS)
    greet(after // SUBS, after % SUBS)
    greet(before // SUBS, before % SUBS)

    for n in range(SWEEPS + 1):
        states[n, FIELDS:8, :] = jnp.zeros((8 - FIELDS, ROWS), F32)
    for f in range(FIELDS):
        coef[f : f + 1, :] = RELAX / diag[f, f : f + 1, :].astype(F32)
    states[0, 0:FIELDS, :] = rhs[...] * coef[0:FIELDS, :]

    lane = lax.broadcasted_iota(I32, (8, LANES), 1)
    in_use = lane < 64
    for zz in range(GZ):
        pos = (zz * 16 + (lane >> 5) * 8 + (lane & 7)) & 127
        src = jnp.zeros((8, LANES), I32)
        wei = jnp.zeros((8, LANES), F32)
        for yy in range(4):
            mine = ((lane >> 3) & 3) == yy
            src = jnp.where(mine, jnp.take_along_axis(row8(fsrc, yy), pos, axis=1, mode="promise_in_bounds"), src)
            wei = jnp.where(mine, jnp.take_along_axis(row8(fwei, yy), pos, axis=1, mode="promise_in_bounds"), wei)
        fsi[zz] = jnp.where(in_use, src, 0)
        fwt[zz] = jnp.where(in_use, wei, 0.0)
    cell = lax.broadcasted_iota(I32, (512, LANES), 0)
    for rr in range(GR):
        pos = ((lane >> 3) * 16 + (rr // 4) * 8 + (lane & 7)) & 127
        don = jnp.take_along_axis(row8(fdon, rr % 4), pos, axis=1, mode="promise_in_bounds")
        don = jnp.where(in_use, don, -1)[0:1, :]
        don1h[:, rr * LANES : (rr + 1) * LANES] = jnp.where(cell == don, 1.0, 0.0).astype(BF16)
    spot = lax.broadcasted_iota(I32, (256, LANES), 0)
    for e in range(WARP_CHUNKS):
        node = wnode[e : e + 1, :]
        low1h[:, e * LANES : (e + 1) * LANES] = jnp.where(spot == (node & 255), 1.0, 0.0).astype(BF16)
    high = wnode[...] >> 8
    whi[...] = (high & 7) * 4 + (high >> 3)

    pl.semaphore_wait(barrier, (GZ - 1) + (GR * SUBS - 1) + 2)

    def send(src, dst, s_sem, r_sem, b, s):
        pltpu.make_async_remote_copy(
            src_ref=src, dst_ref=dst, send_sem=s_sem, recv_sem=r_sem, device_id=(b, s), device_id_type=MESH
        ).start()

    def drain(ref, sem):
        pltpu.make_async_copy(ref, ref, sem).wait()

    def sweep(n, recv1, recv2):
        send(states.at[n, :, pl.ds(256, 256)], rims.at[n, 0], sem_sr.at[n], sem_rl.at[n], after // SUBS, after % SUBS)
        send(states.at[n, :, pl.ds(0, 256)], rims.at[n, 1], sem_sr.at[n], sem_ru.at[n], before // SUBS, before % SUBS)
        own = [states[n, :, c * LANES : (c + 1) * LANES] for c in range(CHUNKS)]
        for j in range(GZ):
            zt = (z + j) % GZ
            idx = fsi[zt]
            out = lane_pick(own, 0, idx & 127, idx >> 7) * fwt[zt]
            if j == 0:
                recv1[z, :, 0:256] = states[n, :, 512:768]
                recv1[z, :, 256:384] = out
            else:
                send1[n, j - 1, :, 0:256] = states[n, :, 512:768]
                send1[n, j - 1, :, 256:384] = out
                send(send1.at[n, j - 1], recv1.at[z], sem_s1.at[n], sem_r1.at[n], blk_of(zt, r), sub)
        drain(send1.at[n], sem_r1.at[n])

        came = [recv1[zz, :, 256:384] for zz in range(GZ)]
        for rr in range(GR):
            out = jnp.zeros((8, LANES), F32)
            for zz in range(GZ):
                shift = ((zz - rr) * 8) % LANES
                moved = pltpu.roll(came[zz], shift, 1) if shift else came[zz]
                out = jnp.where((lane >> 3) == zz, moved, out)
            send2[n, rr, :, 256:384] = out
        for j in range(GR):
            rt = (r + j) % GR
            bt = blk_of(z, rt)
            block = recv1[(partner[bt] // 2) % GZ, :, 0:256]
            if j == 0:
                recv2[r, :, 0:256] = block
                recv2[r, :, 256:384] = send2[n, r, :, 256:384]
            else:
                send2[n, rt, :, 0:256] = block
                send(send2.at[n, rt], recv2.at[r], sem_s2.at[n], sem_r2.at[n], bt, sub)

        drain(rims.at[n, 0], sem_rl.at[n])
        drain(rims.at[n, 1], sem_ru.at[n])
        lower = [jnp.where(dev == 0, 0.0, rims[n, 0, :, c * LANES : (c + 1) * LANES]) for c in range(2)]
        upper = [jnp.where(dev == DEVICES - 1, 0.0, rims[n, 1, :, c * LANES : (c + 1) * LANES]) for c in range(2)]
        near = lower + own + upper

        def add_blocks(total, c, sources, first):
            at = slice(c * LANES, (c + 1) * LANES)
            for k in range(NEIGH):
                idx = row8(nbr, k, c * LANES)
                pick = lane_pick(sources, first, idx & 127, idx >> 7)
                for f in range(FIELDS):
                    total = total + jac[k, f, :, at].astype(F32) * pick[f : f + 1, :]
            return total

        for c in range(CHUNKS):
            at = slice(c * LANES, (c + 1) * LANES)
            total = jnp.zeros((FIELDS, LANES), F32)
            for f in range(FIELDS):
                total = total + diag[f, :, at].astype(F32) * own[c][f : f + 1, :]
            image[0:FIELDS, at] = add_blocks(total, c, near, 0)

        drain(send2.at[n, pl.ds(0, GR - 1)], sem_r2.at[n])
        mate = partner[blk]
        slot = (mate % 2) * 4 + mate // 16
        far = [recv2[slot, :, c * LANES : (c + 1) * LANES] for c in range(2)]
        arrived = jnp.concatenate([recv2[rr, :, 256:384] for rr in range(GR)], axis=1)
        parts = dot_nt(jnp.concatenate(split3(arrived), axis=0).astype(BF16), don1h[...])
        fringe = parts[0:8] + parts[8:16] + parts[16:24]
        for c in range(CHUNKS):
            at = slice(c * LANES, (c + 1) * LANES)
            total = add_blocks(image[0:FIELDS, at], c, far, 10)
            if c < 4:
                total = total - fringe[0:FIELDS, at]
            states[n + 1, 0:FIELDS, at] = own[c][0:FIELDS] + (rhs[:, at] - total) * coef[0:FIELDS, at]

    for n, hops in enumerate(((recv1_0, recv2_0), (recv1_1, recv2_1), (recv1_2, recv2_2))):
        sweep(n, *hops)

    final = states[SWEEPS, 0:FIELDS, :]
    out_state[...] = final
    volume[...] = jnp.zeros((8, ROWS), F32)
    for c in range(3):
        volume[c : c + 1, :] = jnp.sum(metric[c].astype(F32) * final, axis=0, keepdims=True)
    vol = [volume[:, c * LANES : (c + 1) * LANES] for c in range(CHUNKS)]
    hi_row = lax.broadcasted_iota(I32, (32, LANES), 0)
    for e in range(WARP_CHUNKS):
        at = slice(e * LANES, (e + 1) * LANES)
        idx = row8(wrow, e)
        terms = lane_pick(vol, 0, idx & 127, idx >> 7) * row8(wwei, e)
        here = hi_row == whi[e : e + 1, :]
        for p, part in enumerate(split3(terms)):
            for c in range(3):
                row = (p * 3 + c) * 32
                spread[row : row + 32, at] = jnp.where(here, part[c : c + 1, :], 0.0).astype(BF16)
    dense = dot_nt(spread[...], low1h[...])
    dense = dense[0:96] + dense[96:192] + dense[192:288]
    for zz in range(GZ):
        for c in range(3):
            row = c * 32 + zz * 4
            send_a[zz, c, 0:4, :] = dense[row : row + 4, 0:LANES]
            send_a[zz, c, 4:8, :] = dense[row : row + 4, LANES : 2 * LANES]
    recv_a[z] = send_a[z]
    for j in range(1, GZ):
        zt = (z + j) % GZ
        send(send_a.at[zt], recv_a.at[z], sem_fin.at[0], sem_fin.at[1], blk_of(zt, r), sub)
    drain(send_a.at[pl.ds(0, GZ - 1)], sem_fin.at[1])
    total = recv_a[0]
    for zz in range(1, GZ):
        total = total + recv_a[zz]
    for rr in range(GR):
        for c in range(3):
            send_b[rr, c : c + 1, :] = total[c, rr : rr + 1, :]
    recv_b[r * SUBS + sub] = send_b[r]
    for j in range(1, GR * SUBS):
        rt = (r + j // SUBS) % GR
        send(send_b.at[rt], recv_b.at[r * SUBS + sub], sem_fin.at[2], sem_fin.at[3], blk_of(z, rt), (sub + j % SUBS) % SUBS)
    drain(recv_b.at[pl.ds(0, GR * SUBS - 1)], sem_fin.at[3])
    surf = recv_b[0]
    for n in range(1, GR * SUBS):
        surf = surf + recv_b[n]
    out_surf[...] = surf

    for n in range(SWEEPS):
        drain(send1.at[n], sem_s1.at[n])
        drain(send2.at[n, pl.ds(0, GR - 1)], sem_s2.at[n])
        drain(rims.at[n], sem_sr.at[n])
    drain(send_a.at[pl.ds(0, GZ - 1)], sem_fin.at[0])
    drain(recv_b.at[pl.ds(0, GR * SUBS - 1)], sem_fin.at[2])


def body(
    residual_rhs, diag_blocks, jacobian_blocks, neighbors, partner, fringe_source, fringe_weight, fringe_donor,
    metric_sens, warp_row, warp_node, warp_weight,
):
    vmem = pl.BlockSpec(memory_space=pltpu.VMEM)
    smem = pl.BlockSpec(memory_space=pltpu.SMEM)
    v = pltpu.VMEM
    dma = pltpu.SemaphoreType.DMA
    return pl.pallas_call(
        kernel,
        out_shape=(
            jax.ShapeDtypeStruct((FIELDS, ROWS), F32),
            jax.ShapeDtypeStruct((3, LANES), F32),
        ),
        in_specs=[vmem] * 4 + [smem] + [vmem] * 7,
        out_specs=(vmem, vmem),
        scratch_shapes=[
            v((SWEEPS + 1, 8, ROWS), F32),
            v((8, ROWS), F32),
            v((8, ROWS), F32),
            v((GZ, 8, LANES), I32),
            v((GZ, 8, LANES), F32),
            v((512, GR * LANES), BF16),
            v((256, WARP_CHUNKS * LANES), BF16),
            v((WARP_CHUNKS, LANES), I32),
            v((SWEEPS, GZ - 1, 8, 384), F32),
            v((GZ, 8, 384), F32),
            v((GZ, 8, 384), F32),
            v((GZ, 8, 384), F32),
            v((SWEEPS, GR, 8, 384), F32),
            v((GR, 8, 384), F32),
            v((GR, 8, 384), F32),
            v((GR, 8, 384), F32),
            v((SWEEPS, 2, 8, RIM), F32),
            v((8, ROWS), F32),
            v((288, WARP_CHUNKS * LANES), BF16),
            v((GZ, 3, 8, LANES), F32),
            v((GZ, 3, 8, LANES), F32),
            v((GR, 3, LANES), F32),
            v((GR * SUBS, 3, LANES), F32),
        ]
        + [dma((SWEEPS,))] * 7
        + [dma((4,))],
        compiler_params=pltpu.CompilerParams(
            collective_id=0, has_side_effects=True, vmem_limit_bytes=40 * 1024 * 1024
        ),
    )(
        residual_rhs,
        diag_blocks,
        jacobian_blocks,
        neighbors,
        partner,
        fringe_source.reshape(4, LANES),
        fringe_weight.reshape(4, LANES),
        fringe_donor.reshape(4, LANES),
        metric_sens,
        warp_row.reshape(WARP_CHUNKS, LANES),
        warp_node.reshape(WARP_CHUNKS, LANES),
        warp_weight.reshape(WARP_CHUNKS, LANES),
    )


def solution(mesh):
    both = ("blk", "sub")
    in_specs = (
        P(None, both),
        P(None, None, both),
        P(None, None, None, both),
        P(None, both),
        P(),
        P(both),
        P(both),
        P(both),
        P(None, None, both),
        P(both),
        P(both),
        P(both),
    )
    out_specs = (P(None, both), P(None, "blk"))
    return jax.shard_map(body, mesh=mesh, in_specs=in_specs, out_specs=out_specs, check_vma=False)
```

time: 707 us -> 61.7 us (0.09); the launches traced: 697 us -> 61.2 us
  waiting for transfers between devices: 265 us -> 0 us
  blocking collectives: 174 us -> 0 us
  local copies, waits for them, and re-layouts: 114 us -> 8.76 us
  other arithmetic: 63.8 us -> 0 us
  starting transfers between devices: 63.6 us -> 0 us
  Pallas kernels: 0 us -> 51.7 us
  between operations: 17.5 us -> 0.68 us
    psum x1 -> x0, waiting for transfers between devices: 265 us -> none  [body(): total = lax.psum(dense, ('blk', 'sub'))]
    all_gather x3 -> x0, blocking collectives: 174 us -> none  [body(): every = lax.all_gather(migrants, 'blk', axis=1, tiled=True)]
    slice x77 -> x0, local copies, waits for them, and re-layouts: 67.8 us -> none  [the longest x38 25.7 us: body(): jacobian_blocks[k, apply_f].astype(jnp.float32) * picked[apply_f][None, :]]
    pallas_call x0 -> x1, Pallas kernels: none -> 51.7 us  [body(): pl.pallas_call(kernel, out_shape=(jax.ShapeDtypeStruct((FIELDS, ROWS), F3...]
    all_to_all x3 -> x0, starting transfers between devices: 42.3 us -> none  [body(): lax.all_to_all(outgoing, 'blk', split_axis=1, concat_axis=1, tiled=True)]
    gather x21 -> x0, local copies, waits for them, and re-layouts: 38.9 us -> none  [the longest x18 35.8 us: body(): picked = window[:, neighbors[k]]]
    scatter-add x4 -> x0, other arithmetic: 32.4 us -> none  [the longest x1 20.1 us: body(): jnp.zeros((3, groups * NODE_BLK), jnp.float32).at[:, warp_node].add(terms)]
    add x7 -> x0, other arithmetic: 25.3 us -> none  [the longest x3 24.2 us: body(): image + jacobian_blocks[k, apply_f].astype(jnp.float32) * picked[apply_f]...]
  transfers between devices with their start and end apart: 10 -> 0, of which waited for: 1 -> 0; matrix products, arithmetic and copies ran while one was open for 19% -> 0% of each run, Pallas kernels for 0% -> 0%
where the time goes in v1:
time: 61.7 us; the launch traced here: 61.2 us
  Pallas kernels  51.7 us (84%)
  local copies, waits for them, and re-layouts  8.76 us (14%)
  between operations  0.68 us (1%)
    pallas_call x1, Pallas kernels, body(): pl.pallas_call(kernel, out_shape=(jax.ShapeDtypeStruct((FIELDS, ROWS), F3...  51.7 us
    unnamed x26, local copies, waits for them, and re-layouts  8.76 us

profile of v1, /device:TPU:1, one launch (start us, length us, event | category | flops | bytes accessed | tf_op | source)
XLA Modules:
  0.0 61.2 jit_solution(2435340117073241684)
XLA Ops:
  0.6 0.0 copy-start.5
  0.6 0.0 copy-start.8
  0.7 0.0 copy-start.11
  0.7 0.7 %copy-done.5 = s32[2048]{0:T(1024)S(1)} copy-done((s32[2048]{0:T(1024)S(1)}, s32[2048]{0:T(1024)}, u32[]{:S(2)}) %copy-start.5) | copy-done | bytes 8216
  1.3 0.0 copy-done.8
  1.3 0.0 copy-done.11
  1.3 0.0 copy-start
  1.3 1.0 %copy-done = bf16[6,6,6,768]{3,2,1,0:T(8,128)(2,1)S(1)} copy-done((bf16[6,6,6,768]{3,2,1,0:T(8,128)(2,1)S(1)}, bf16[6,6,6,768]{3,2,1,0:T(8,128)(2,1)}, u32[]{:S(2)}) %copy-start) | copy-done | bytes 331800
  2.4 0.0 copy-start.1
  2.4 0.9 %copy-done.1 = bf16[6,6,768]{2,1,0:T(8,128)(2,1)S(1)} copy-done((bf16[6,6,768]{2,1,0:T(8,128)(2,1)S(1)}, bf16[6,6,768]{2,1,0:T(8,128)(2,1)}, u32[]{:S(2)}) %copy-start.1) | copy-done | bytes 55320
  3.2 0.0 copy-start.2
  3.2 0.8 %copy-done.2 = bf16[3,6,768]{2,1,0:T(8,128)(2,1)S(1)} copy-done((bf16[3,6,768]{2,1,0:T(8,128)(2,1)S(1)}, bf16[3,6,768]{2,1,0:T(8,128)(2,1)}, u32[]{:S(2)}) %copy-start.2) | copy-done | bytes 27672
  4.0 0.0 copy-start.3
  4.0 0.7 %copy-done.3 = f32[6,768]{1,0:T(8,128)S(1)} copy-done((f32[6,768]{1,0:T(8,128)S(1)}, f32[6,768]{1,0:T(8,128)}, u32[]{:S(2)}) %copy-start.3) | copy-done | bytes 18456
  4.7 0.0 copy-start.4
  4.7 0.7 %copy-done.4 = s32[6,768]{1,0:T(8,128)S(1)} copy-done((s32[6,768]{1,0:T(8,128)S(1)}, s32[6,768]{1,0:T(8,128)}, u32[]{:S(2)}) %copy-start.4) | copy-done | bytes 18456
  5.5 0.0 copy-start.6
  5.5 0.7 %copy-done.6 = s32[2048]{0:T(1024)S(1)} copy-done((s32[2048]{0:T(1024)S(1)}, s32[2048]{0:T(1024)}, u32[]{:S(2)}) %copy-start.6) | copy-done | bytes 8216
  6.2 0.0 copy-start.7
  6.2 0.7 %copy-done.7 = f32[2048]{0:T(1024)S(1)} copy-done((f32[2048]{0:T(1024)S(1)}, f32[2048]{0:T(1024)}, u32[]{:S(2)}) %copy-start.7) | copy-done | bytes 8216
  6.9 0.0 copy-start.9
  6.9 0.7 %copy-done.9 = f32[512]{0:T(512)S(1)} copy-done((f32[512]{0:T(512)S(1)}, f32[512]{0:T(512)}, u32[]{:S(2)}) %copy-start.9) | copy-done | bytes 2072
  7.6 0.0 copy-start.10
  7.6 0.7 %copy-done.10 = s32[512]{0:T(512)S(1)} copy-done((s32[512]{0:T(512)S(1)}, s32[512]{0:T(512)}, u32[]{:S(2)}) %copy-start.10) | copy-done | bytes 2072
  8.2 51.7 %shard_map.131 = (f32[6,768]{1,0:T(8,128)S(1)}, f32[3,128]{1,0:T(4,128)S(1)}) custom-call(f32[6,768]{1,0:T(8,128)S(1)} %copy-done.3, bf16[6,6,768]{2,1,0:T(8,128)(2,1)S(1)} %copy-done.1, bf16[6,6,6,768]{3,2,1,0:T(8,128)(2,1)S(1)} %copy-done, s32[6,768]{1,0:T(8,128)S(1)} %copy-done.4, s32[64]{0:T(128)S(1)} %copy-done.11, s32[4,128]{1,0:T(4,128)S(1)} %bitcast.9, ...), custom_call_target="tpu_custom_call" | custom-call | tf_op jit(solution)/shard_map/pallas_call | solution.py:253
  60.0 0.6 copy.16
  60.6 0.6 copy.17
Async XLA Ops:
  0.6 0.7 %copy-start.5 = (s32[2048]{0:T(1024)S(1)}, s32[2048]{0:T(1024)}, u32[]{:S(2)}) copy-start(s32[2048]{0:T(1024)} %param.21) | copy-start | bytes 24580
  0.6 0.7 %copy-start.8 = (s32[512]{0:T(512)S(1)}, s32[512]{0:T(512)}, u32[]{:S(2)}) copy-start(s32[512]{0:T(512)} %param.17) | copy-start | bytes 6148
  0.7 0.7 %copy-start.11 = (s32[64]{0:T(128)S(1)}, s32[64]{0:T(128)}, u32[]{:S(2)}) copy-start(s32[64]{0:T(128)} %partner.1) | copy-start | bytes 772
  1.3 1.0 %copy-start = (bf16[6,6,6,768]{3,2,1,0:T(8,128)(2,1)S(1)}, bf16[6,6,6,768]{3,2,1,0:T(8,128)(2,1)}, u32[]{:S(2)}) copy-start(bf16[6,6,6,768]{3,2,1,0:T(8,128)(2,1)} %jac.1) | copy-start | bytes 995332
  2.4 0.9 %copy-start.1 = (bf16[6,6,768]{2,1,0:T(8,128)(2,1)S(1)}, bf16[6,6,768]{2,1,0:T(8,128)(2,1)}, u32[]{:S(2)}) copy-start(bf16[6,6,768]{2,1,0:T(8,128)(2,1)} %diag.1) | copy-start | bytes 165892
  3.2 0.8 %copy-start.2 = (bf16[3,6,768]{2,1,0:T(8,128)(2,1)S(1)}, bf16[3,6,768]{2,1,0:T(8,128)(2,1)}, u32[]{:S(2)}) copy-start(bf16[3,6,768]{2,1,0:T(8,128)(2,1)} %metric.1) | copy-start | bytes 82948
  4.0 0.7 %copy-start.3 = (f32[6,768]{1,0:T(8,128)S(1)}, f32[6,768]{1,0:T(8,128)}, u32[]{:S(2)}) copy-start(f32[6,768]{1,0:T(8,128)} %rhs.1) | copy-start | bytes 55300
  4.7 0.7 %copy-start.4 = (s32[6,768]{1,0:T(8,128)S(1)}, s32[6,768]{1,0:T(8,128)}, u32[]{:S(2)}) copy-start(s32[6,768]{1,0:T(8,128)} %nbr.1) | copy-start | bytes 55300
  5.5 0.7 %copy-start.6 = (s32[2048]{0:T(1024)S(1)}, s32[2048]{0:T(1024)}, u32[]{:S(2)}) copy-start(s32[2048]{0:T(1024)} %param.22) | copy-start | bytes 24580
  6.2 0.7 %copy-start.7 = (f32[2048]{0:T(1024)S(1)}, f32[2048]{0:T(1024)}, u32[]{:S(2)}) copy-start(f32[2048]{0:T(1024)} %param.23) | copy-start | bytes 24580
  6.9 0.7 %copy-start.9 = (f32[512]{0:T(512)S(1)}, f32[512]{0:T(512)}, u32[]{:S(2)}) copy-start(f32[512]{0:T(512)} %param.18) | copy-start | bytes 6148
  7.6 0.7 %copy-start.10 = (s32[512]{0:T(512)S(1)}, s32[512]{0:T(512)}, u32[]{:S(2)}) copy-start(s32[512]{0:T(512)} %param.19) | copy-start | bytes 6148

commit v2 on v1

v2 whole, which is shorter than its diff:
```python
import jax
import jax.numpy as jnp
from jax import lax
from jax.experimental import pallas as pl
from jax.experimental.pallas import tpu as pltpu
from jax.sharding import PartitionSpec as P

MESH = pl.DeviceIdType.MESH
F32, BF16, I32 = jnp.float32, jnp.bfloat16, jnp.int32

FIELDS = 6
NEIGH = 6
SWEEPS = 3
ROWS = 768
CHUNKS = 6
RIM = 256
LANES = 128
GZ = 8
GR = 8
SUBS = 4
DEVICES = 256
WARP_CHUNKS = 16
RELAX = 0.8
FAR_FIRST = (4, 3, 5, 2, 6, 1, 7)


def split2(v):
    a = v.astype(BF16).astype(F32)
    return a, (v - a).astype(BF16).astype(F32)


def take(values, index):
    return jnp.take_along_axis(values, index, axis=1, mode="promise_in_bounds")


def lane_pick(sources, first, low, high, acc=None):
    acc = jnp.zeros((8, LANES), F32) if acc is None else acc
    for n, src in enumerate(sources):
        acc = jnp.where(high == first + n, take(src, low), acc)
    return acc


def row8(ref, i, start=0):
    return jnp.broadcast_to(ref[i : i + 1, start : start + LANES], (8, LANES))


def dot_nt(a, b):
    return lax.dot_general(a, b, (((1,), (1,)), ((), ())), preferred_element_type=F32)


def kernel(
    h_rhs, h_diag, h_jac, h_nbr, h_partner, h_fsrc, h_fwei, h_fdon, h_metric, h_wrow, h_wnode, h_wwei,
    out_state, out_surf,
    rhs, diag, jac, nbr, partner, fsrc, fwei, fdon, metric, wrow, wnode, wwei,
    states, coef, picks, blocks, fsi, fwt, don1h, low1h, whi,
    mates1_0, mates1_1, mates1_2, fwd, mates2_0, mates2_1, mates2_2,
    fsend1, frecv1, fsend2, frecv2, rims,
    volume, spread, send_a, recv_a, send_b, recv_b,
    sem_in, sem_m1s, sem_m1r, sem_m2s, sem_m2r, sem_f1s, sem_f1r, sem_f2s, sem_f2r, sem_sr, sem_rl, sem_ru, sem_fin,
):
    blk, sub = lax.axis_index("blk"), lax.axis_index("sub")
    y, z, core = blk // 16, (blk // 2) % GZ, blk % 2
    r = core * 4 + y
    dev = blk * SUBS + sub
    after, before = (dev + 1) % DEVICES, (dev + DEVICES - 1) % DEVICES
    mates1 = (mates1_0, mates1_1, mates1_2)
    mates2 = (mates2_0, mates2_1, mates2_2)

    def blk_of(zz, rr):
        return (rr % 4) * 16 + zz * 2 + rr // 4

    barrier = pltpu.get_barrier_semaphore()

    def greet(b, s):
        pl.semaphore_signal(barrier, inc=1, device_id=(b, s), device_id_type=MESH)

    for j in range(1, GZ):
        greet(blk_of((z + j) % GZ, r), sub)
    for j in range(1, GR * SUBS):
        greet(blk_of(z, (r + j // SUBS) % GR), (sub + j % SUBS) % SUBS)
    greet(after // SUBS, after % SUBS)
    greet(before // SUBS, before % SUBS)

    pairs = dict(
        rhs=(h_rhs, rhs), diag=(h_diag, diag), fsrc=(h_fsrc, fsrc), fwei=(h_fwei, fwei), partner=(h_partner, partner),
        jac=(h_jac, jac), nbr=(h_nbr, nbr), fdon=(h_fdon, fdon), wnode=(h_wnode, wnode), metric=(h_metric, metric),
        wrow=(h_wrow, wrow), wwei=(h_wwei, wwei),
    )
    fetch = {name: pltpu.make_async_copy(*pair, sem_in.at[n]) for n, (name, pair) in enumerate(pairs.items())}
    for copy in fetch.values():
        copy.start()

    for n in range(SWEEPS + 1):
        states[n, FIELDS:8, :] = jnp.zeros((8 - FIELDS, ROWS), F32)

    fetch["rhs"].wait()
    fetch["diag"].wait()
    for f in range(FIELDS):
        coef[f : f + 1, :] = RELAX / diag[f, f : f + 1, :].astype(F32)
    states[0, 0:FIELDS, :] = rhs[...] * coef[0:FIELDS, :]

    lane = lax.broadcasted_iota(I32, (8, LANES), 1)
    fetch["fsrc"].wait()
    fetch["fwei"].wait()
    for zz in range(GZ // 2):
        pos = zz * 32 + (lane >> 6) * 16 + ((lane >> 5) & 1) * 8 + (lane & 7)
        src = jnp.zeros((8, LANES), I32)
        wei = jnp.zeros((8, LANES), F32)
        for yy in range(4):
            mine = ((lane >> 3) & 3) == yy
            src = jnp.where(mine, take(row8(fsrc, yy), pos), src)
            wei = jnp.where(mine, take(row8(fwei, yy), pos), wei)
        fsi[zz] = src
        fwt[zz] = wei
    fetch["partner"].wait()
    fetch["nbr"].wait()
    fetch["jac"].wait()
    for k in range(NEIGH):
        for f in range(FIELDS):
            blocks[k * FIELDS + f, 0:FIELDS, :] = jac[k, f].astype(F32)

    pl.semaphore_wait(barrier, (GZ - 1) + (GR * SUBS - 1) + 2)

    def send(src, dst, s_sem, r_sem, b, s):
        pltpu.make_async_remote_copy(
            src_ref=src, dst_ref=dst, send_sem=s_sem, recv_sem=r_sem, device_id=(b, s), device_id_type=MESH
        ).start()

    def drain(ref, sem):
        pltpu.make_async_copy(ref, ref, sem).wait()

    def send_mates(n):
        for j in range(1, GZ):
            zt = (z + FAR_FIRST[j - 1]) % GZ
            send(states.at[n, :, pl.ds(512, 256)], mates1[n].at[z], sem_m1s.at[n], sem_m1r.at[n], blk_of(zt, r), sub)
        mates1[n][z] = states[n, :, 512:768]

    def send_cells(n):
        send(states.at[n, :, pl.ds(256, 256)], rims.at[n, 0], sem_sr.at[n], sem_rl.at[n], after // SUBS, after % SUBS)
        send(states.at[n, :, pl.ds(0, 256)], rims.at[n, 1], sem_sr.at[n], sem_ru.at[n], before // SUBS, before % SUBS)
        own = [states[n, :, c * LANES : (c + 1) * LANES] for c in range(CHUNKS)]
        for zz in range(GZ // 2):
            idx = fsi[zz]
            fsend1[n, zz] = lane_pick(own, 0, idx & 127, idx >> 7) * fwt[zz]
        for j in range(1, GZ):
            zt = (z + FAR_FIRST[j - 1]) % GZ
            send(fsend1.at[n, zt // 2], frecv1.at[n, z], sem_f1s.at[n], sem_f1r.at[n], blk_of(zt, r), sub)
        frecv1[n, z] = fsend1[n, z // 2]

    def pick_own(own):
        for c in range(CHUNKS):
            for k in range(NEIGH):
                idx = row8(nbr, k, c * LANES)
                picks[k, :, c * LANES : (c + 1) * LANES] = lane_pick(own, 2, idx & 127, idx >> 7)

    def pick_rims(lower, upper):
        for c in range(CHUNKS):
            at = slice(c * LANES, (c + 1) * LANES)
            for k in range(NEIGH):
                idx = row8(nbr, k, c * LANES)
                acc = lane_pick(lower, 0, idx & 127, idx >> 7, picks[k, :, at])
                picks[k, :, at] = lane_pick(upper, 8, idx & 127, idx >> 7, acc)

    def finish(n, c, far, fringe):
        at = slice(c * LANES, (c + 1) * LANES)
        sums = []
        for k in range(NEIGH):
            idx = row8(nbr, k, c * LANES)
            pick = lane_pick(far, 10, idx & 127, idx >> 7, picks[k, :, at])
            part = blocks[k * FIELDS, 0:FIELDS, at] * pick[0:1, :]
            for f in range(1, FIELDS):
                part = part + blocks[k * FIELDS + f, 0:FIELDS, at] * pick[f : f + 1, :]
            sums.append(part)
        old = states[n, :, at]
        part = diag[0, :, at].astype(F32) * old[0:1, :]
        for f in range(1, FIELDS):
            part = part + diag[f, :, at].astype(F32) * old[f : f + 1, :]
        total = (sums[0] + sums[1]) + (sums[2] + sums[3]) + (sums[4] + sums[5]) + part
        if fringe is not None:
            total = total - fringe[0:FIELDS, at]
        states[n + 1, 0:FIELDS, at] = old[0:FIELDS] + (rhs[:, at] - total) * coef[0:FIELDS, at]

    send_mates(0)
    send_cells(0)

    fetch["fdon"].wait()
    cell = lax.broadcasted_iota(I32, (512, LANES), 0)
    for rr in range(GR):
        pos = ((lane >> 3) * 16 + (rr // 4) * 8 + (lane & 7)) & 127
        don = jnp.where(lane < 64, take(row8(fdon, rr % 4), pos), -1)[0:1, :]
        don1h[:, rr * LANES : (rr + 1) * LANES] = jnp.where(cell == don, 1.0, 0.0).astype(BF16)
    fetch["wnode"].wait()
    spot = lax.broadcasted_iota(I32, (512, LANES), 0)
    for e in range(WARP_CHUNKS):
        node = wnode[e : e + 1, :]
        low1h[:, e * LANES : (e + 1) * LANES] = jnp.where(spot == (node & 511), 1.0, 0.0).astype(BF16)
    high = wnode[...] >> 9
    whi[...] = (high & 3) * 4 + (high >> 2)

    for n in range(SWEEPS):
        own = [states[n, :, c * LANES : (c + 1) * LANES] for c in range(CHUNKS)]
        pick_own(own)

        drain(mates1[n].at[pl.ds(0, GZ - 1)], sem_m1r.at[n])
        for j in range(GR):
            rt = (r + j) % GR
            bt = blk_of(z, rt)
            block = mates1[n][(partner[bt] // 2) % GZ]
            if j == 0:
                mates2[n][r] = block
            else:
                fwd[n, rt] = block
                send(fwd.at[n, rt], mates2[n].at[r], sem_m2s.at[n], sem_m2r.at[n], bt, sub)

        drain(frecv1.at[n, pl.ds(0, GZ - 1)], sem_f1r.at[n])
        odd = z % 2 == 1
        came = []
        for zz in range(GZ):
            v = frecv1[n, zz]
            came.append(jnp.where(odd, pltpu.roll(v, 64, 1), v))
        for rr in range(GR):
            out = jnp.zeros((8, LANES), F32)
            for zz in range(GZ):
                shift = ((zz - rr) * 8) % LANES
                moved = pltpu.roll(came[zz], shift, 1) if shift else came[zz]
                out = jnp.where((lane >> 3) == zz, moved, out)
            fsend2[n, rr] = out
        for j in range(1, GR):
            rt = (r + j) % GR
            send(fsend2.at[n, rt], frecv2.at[n, r], sem_f2s.at[n], sem_f2r.at[n], blk_of(z, rt), sub)
        frecv2[n, r] = fsend2[n, r]

        drain(rims.at[n, 0], sem_rl.at[n])
        drain(rims.at[n, 1], sem_ru.at[n])
        lower = [jnp.where(dev == 0, 0.0, rims[n, 0, :, c * LANES : (c + 1) * LANES]) for c in range(2)]
        upper = [jnp.where(dev == DEVICES - 1, 0.0, rims[n, 1, :, c * LANES : (c + 1) * LANES]) for c in range(2)]
        pick_rims(lower, upper)

        drain(mates2[n].at[pl.ds(0, GR - 1)], sem_m2r.at[n])
        mate = partner[blk]
        slot = (mate % 2) * 4 + mate // 16
        far = [mates2[n][slot, :, c * LANES : (c + 1) * LANES] for c in range(2)]
        for c in range(4, CHUNKS):
            finish(n, c, far, None)
        if n + 1 < SWEEPS:
            send_mates(n + 1)
        drain(frecv2.at[n, pl.ds(0, GR - 1)], sem_f2r.at[n])
        arrived = jnp.concatenate([frecv2[n, rr] for rr in range(GR)], axis=1)
        parts = dot_nt(jnp.concatenate(split2(arrived), axis=0).astype(BF16), don1h[...])
        fringe = parts[0:8] + parts[8:16]
        for c in range(4):
            finish(n, c, far, fringe)
        if n + 1 < SWEEPS:
            send_cells(n + 1)

    final = states[SWEEPS, 0:FIELDS, :]
    out_state[...] = final
    fetch["metric"].wait()
    fetch["wrow"].wait()
    fetch["wwei"].wait()
    volume[...] = jnp.zeros((8, ROWS), F32)
    for c in range(3):
        volume[c : c + 1, :] = jnp.sum(metric[c].astype(F32) * final, axis=0, keepdims=True)
    vol = [volume[:, c * LANES : (c + 1) * LANES] for c in range(CHUNKS)]
    hi_row = lax.broadcasted_iota(I32, (16, LANES), 0)
    for e in range(WARP_CHUNKS):
        at = slice(e * LANES, (e + 1) * LANES)
        idx = row8(wrow, e)
        terms = lane_pick(vol, 0, idx & 127, idx >> 7) * row8(wwei, e)
        here = hi_row == whi[e : e + 1, :]
        for p, part in enumerate(split2(terms)):
            for c in range(3):
                row = (p * 3 + c) * 16
                spread[row : row + 16, at] = jnp.where(here, part[c : c + 1, :], 0.0).astype(BF16)
    dense = dot_nt(spread[...], low1h[...])
    dense = dense[0:48] + dense[48:96]
    for zz in range(GZ):
        for c in range(3):
            row = c * 16 + (zz // 2) * 4
            col = (zz % 2) * 256
            send_a[zz, c, 0:4, :] = dense[row : row + 4, col : col + LANES]
            send_a[zz, c, 4:8, :] = dense[row : row + 4, col + LANES : col + 2 * LANES]
    for j in range(1, GZ):
        zt = (z + FAR_FIRST[j - 1]) % GZ
        send(send_a.at[zt], recv_a.at[z], sem_fin.at[0], sem_fin.at[1], blk_of(zt, r), sub)
    recv_a[z] = send_a[z]
    drain(send_a.at[pl.ds(0, GZ - 1)], sem_fin.at[1])
    total = recv_a[0]
    for zz in range(1, GZ):
        total = total + recv_a[zz]
    for rr in range(GR):
        for c in range(3):
            send_b[rr, c : c + 1, :] = total[c, rr : rr + 1, :]
    for j in range(1, GR * SUBS):
        rt = (r + j // SUBS) % GR
        send(send_b.at[rt], recv_b.at[r * SUBS + sub], sem_fin.at[2], sem_fin.at[3], blk_of(z, rt), (sub + j % SUBS) % SUBS)
    recv_b[r * SUBS + sub] = send_b[r]
    drain(recv_b.at[pl.ds(0, GR * SUBS - 1)], sem_fin.at[3])
    surf = recv_b[0]
    for n in range(1, GR * SUBS):
        surf = surf + recv_b[n]
    out_surf[...] = surf

    for n in range(SWEEPS):
        drain(mates1[n].at[pl.ds(0, GZ - 1)], sem_m1s.at[n])
        drain(fwd.at[n, pl.ds(0, GR - 1)], sem_m2s.at[n])
        drain(frecv1.at[n, pl.ds(0, GZ - 1)], sem_f1s.at[n])
        drain(fsend2.at[n, pl.ds(0, GR - 1)], sem_f2s.at[n])
        drain(rims.at[n], sem_sr.at[n])
    drain(send_a.at[pl.ds(0, GZ - 1)], sem_fin.at[0])
    drain(recv_b.at[pl.ds(0, GR * SUBS - 1)], sem_fin.at[2])


def body(
    residual_rhs, diag_blocks, jacobian_blocks, neighbors, partner, fringe_source, fringe_weight, fringe_donor,
    metric_sens, warp_row, warp_node, warp_weight,
):
    vmem = pl.BlockSpec(memory_space=pltpu.VMEM)
    hbm = pl.BlockSpec(memory_space=pltpu.HBM)
    v = pltpu.VMEM
    dma = pltpu.SemaphoreType.DMA
    operands = (
        residual_rhs,
        diag_blocks,
        jacobian_blocks,
        neighbors,
        partner,
        fringe_source.reshape(4, LANES),
        fringe_weight.reshape(4, LANES),
        fringe_donor.reshape(4, LANES),
        metric_sens,
        warp_row.reshape(WARP_CHUNKS, LANES),
        warp_node.reshape(WARP_CHUNKS, LANES),
        warp_weight.reshape(WARP_CHUNKS, LANES),
    )
    return pl.pallas_call(
        kernel,
        out_shape=(
            jax.ShapeDtypeStruct((FIELDS, ROWS), F32),
            jax.ShapeDtypeStruct((3, LANES), F32),
        ),
        in_specs=[hbm] * 12,
        out_specs=(vmem, vmem),
        scratch_shapes=[(pltpu.SMEM if n == 4 else v)(o.shape, o.dtype) for n, o in enumerate(operands)]
        + [
            v((SWEEPS + 1, 8, ROWS), F32),
            v((8, ROWS), F32),
            v((NEIGH, 8, ROWS), F32),
            v((NEIGH * FIELDS, 8, ROWS), F32),
            v((GZ // 2, 8, LANES), I32),
            v((GZ // 2, 8, LANES), F32),
            v((512, GR * LANES), BF16),
            v((512, WARP_CHUNKS * LANES), BF16),
            v((WARP_CHUNKS, LANES), I32),
        ]
        + [v((GZ, 8, 256), F32)] * SWEEPS
        + [v((SWEEPS, GR, 8, 256), F32)]
        + [v((GR, 8, 256), F32)] * SWEEPS
        + [
            v((SWEEPS, GZ // 2, 8, LANES), F32),
            v((SWEEPS, GZ, 8, LANES), F32),
            v((SWEEPS, GR, 8, LANES), F32),
            v((SWEEPS, GR, 8, LANES), F32),
            v((SWEEPS, 2, 8, RIM), F32),
            v((8, ROWS), F32),
            v((96, WARP_CHUNKS * LANES), BF16),
            v((GZ, 3, 8, LANES), F32),
            v((GZ, 3, 8, LANES), F32),
            v((GR, 3, LANES), F32),
            v((GR * SUBS, 3, LANES), F32),
        ]
        + [dma((12,))]
        + [dma((SWEEPS,))] * 11
        + [dma((4,))],
        compiler_params=pltpu.CompilerParams(
            collective_id=0, has_side_effects=True, vmem_limit_bytes=60 * 1024 * 1024
        ),
    )(*operands)


def solution(mesh):
    both = ("blk", "sub")
    in_specs = (
        P(None, both),
        P(None, None, both),
        P(None, None, None, both),
        P(None, both),
        P(),
        P(both),
        P(both),
        P(both),
        P(None, None, both),
        P(both),
        P(both),
        P(both),
    )
    out_specs = (P(None, both), P(None, "blk"))
    return jax.shard_map(body, mesh=mesh, in_specs=in_specs, out_specs=out_specs, check_vma=False)
```

time: 61.7 us -> 51.8 us (0.84)
  local copies, waits for them, and re-layouts: 8.76 us -> 1.93 us
  Pallas kernels: 51.7 us -> 49 us
    unnamed x26 -> x4, local copies, waits for them, and re-layouts: 8.76 us -> 1.93 us
    pallas_call x1, Pallas kernels: 51.7 us -> 49 us  [body(): pl.pallas_call(kernel, out_shape=(jax.ShapeDtypeStruct((FIELDS, ROWS), F3...]
where the time goes in v2:
time: 51.8 us; the launch traced here: 51.6 us
  Pallas kernels  49 us (95%)
  local copies, waits for them, and re-layouts  1.93 us (4%)
  between operations  0.65 us (1%)
    pallas_call x1, Pallas kernels, body(): pl.pallas_call(kernel, out_shape=(jax.ShapeDtypeStruct((FIELDS, ROWS), F3...  49 us
    unnamed x4, local copies, waits for them, and re-layouts  1.93 us

profile of v2, /device:TPU:1, one launch (start us, length us, event | category | flops | bytes accessed | tf_op | source)
XLA Modules:
  0.0 51.6 jit_solution(15307209274629566425)
XLA Ops:
  0.6 49.0 %shard_map.131 = (f32[6,768]{1,0:T(8,128)}, f32[3,128]{1,0:T(4,128)}) custom-call(f32[6,768]{1,0:T(8,128)} %h_rhs.1, bf16[6,6,768]{2,1,0:T(8,128)(2,1)} %h_diag.1, bf16[6,6,6,768]{3,2,1,0:T(8,128)(2,1)} %h_jac.1, s32[6,768]{1,0:T(8,128)} %h_nbr.1, s32[64]{0:T(128)} %h_partner.1, s32[4,128]{1,0:T(4,128)} %bitcast.9, f32[4,128]{1,0:T(4,128)} %bitcast.10, ...), custom_call_target="tpu_custom_call" | custom-call | tf_op jit(solution)/shard_map/pallas_call | solution.py:336
  49.7 0.0 copy-start
  49.7 1.3 %copy.16 = f32[6,768]{1,0:T(8,128)} copy(f32[6,768]{1,0:T(8,128)} %get-tuple-element.4) | data formatting | bytes 36864
  51.0 0.0 copy-done
  51.0 0.6 %copy.17 = f32[3,128]{1,0:T(4,128)} copy(f32[3,128]{1,0:T(4,128)S(1)} %copy-done) | data formatting | bytes 3072
Async XLA Ops:
  49.7 1.4 %copy-start = (f32[3,128]{1,0:T(4,128)S(1)}, f32[3,128]{1,0:T(4,128)}, u32[]{:S(2)}) copy-start(f32[3,128]{1,0:T(4,128)} %get-tuple-element.5) | copy-start | bytes 4612
